TPU v7x, 512 devices: a whole 4x4x16 slice. The times are simulated.
512 devices in a mesh: node: 32 (over x, z_hi, core), local: 16 (over z_lo, y).
Axes of the slice: x: 4, y: 4, z: 16 (z_hi: 4, z_lo: 4; z = z_hi * 4 + z_lo), core: 2. Of those that a mesh axis runs over, the one named last changes fastest.
Arguments:
- tokens: bfloat16 [65536, 8192], P(('node', 'local')), may hold values from -24 to 24
- norm_gain: float32 [8192], replicated, may hold values from 0.1 to 1.9
- weight_codes: bfloat16 [2048, 2048], P('local'), may hold values from -6 to 6
- weight_scales: float32 [2048], P('local'), may hold values from 0.004 to 0.04
- key_cotangent: bfloat16 [65536, 512], P(('node', 'local')), may hold values from -6 to 6
Outputs:
- key_states: bfloat16 [65536, 512], P(('node', 'local'))
- token_grad: bfloat16 [65536, 8192], P(('node', 'local'))
- weight_grad: float32 [2048, 2048], P(('node', 'local'))
All inputs are finite; a program needn't handle non-finite values. Where the computation divides by a largest or mean magnitude, that divisor is 1e-20 or more.
Results may differ from a plain program's by a relative error of at most 0.015.
Values may be sent and summed in bfloat16 or wider, within the bound.
A program may use at most 128 MiB of HBM per device.

v0:
```python
import jax
import jax.numpy as jnp
from jax import lax
from jax.sharding import PartitionSpec as P

EPSILON = 1e-05
QUANT_EPS = 1e-06


def for_sending(shard):
    return jax.tree.map(lambda a: a.astype(jnp.bfloat16) if a.dtype == jnp.float32 else a, shard)


def unpack_weight(block_codes, block_scales, kv_width):
    dequantized = block_codes.astype(jnp.float32) * block_scales[:, None]
    return dequantized.astype(jnp.bfloat16).reshape(-1, kv_width)


def quantize(blocks):
    block_scale = jnp.max(jnp.abs(blocks), axis=-1) + QUANT_EPS
    return ((blocks / block_scale[..., None]).astype(jnp.bfloat16), block_scale)


def summed_blocks(received):
    block_codes, block_scale = received
    return jnp.sum(block_codes.astype(jnp.float32) * block_scale[..., None], axis=0)


def body(tokens, norm_gain, weight_codes, weight_scales, key_cotangent):
    kv_width = key_cotangent.shape[1]
    block_rows = weight_codes.shape[1] // kv_width
    node_count = lax.axis_size("node")
    local_count = lax.axis_size("local")
    tok_float = tokens.astype(jnp.float32)
    inv_rms = lax.rsqrt(jnp.mean(tok_float * tok_float, axis=-1, keepdims=True) + EPSILON)
    normed = (tok_float * inv_rms * norm_gain).astype(jnp.bfloat16)
    contract_last = (((1,), (1,)), ((), ()))
    gathered_codes, gathered_scales = (
        lax.all_gather(weight_codes, "local", axis=0, tiled=True),
        lax.all_gather(weight_scales.astype(jnp.bfloat16), "local", axis=0, tiled=True).astype(
            weight_scales.dtype
        ),
    )
    weight = unpack_weight(gathered_codes, gathered_scales, kv_width)
    key_sums = jnp.dot(normed, weight, preferred_element_type=jnp.float32)
    normed_grad = lax.dot_general(
        key_cotangent, weight, contract_last, preferred_element_type=jnp.float32
    )
    key_states = key_sums.astype(jnp.bfloat16)
    scaled_grad = normed_grad * norm_gain
    inner_mean = jnp.mean(tok_float * scaled_grad, axis=-1, keepdims=True)
    token_grad = (inv_rms * (scaled_grad - tok_float * inv_rms * inv_rms * inner_mean)).astype(
        jnp.bfloat16
    )
    partial_grad = lax.dot_general(
        normed, key_cotangent, (((0,), (0,)), ((), ())), preferred_element_type=jnp.float32
    )
    block_width = block_rows * kv_width
    block_count = partial_grad.size // (block_width * node_count * local_count)
    tiled = partial_grad.reshape(1, node_count, local_count, block_count, block_width)
    codes_one, scales_one = quantize(tiled)
    group_sums = summed_blocks(
        (
            lax.all_to_all(codes_one, "local", split_axis=2, concat_axis=0, tiled=True),
            lax.all_to_all(
                scales_one.astype(jnp.bfloat16), "local", split_axis=2, concat_axis=0, tiled=True
            ).astype(scales_one.dtype),
        )
    )
    codes_two, scales_two = quantize(group_sums)
    node_sums = summed_blocks(
        (
            lax.all_to_all(codes_two[None], "node", split_axis=1, concat_axis=0, tiled=True),
            lax.all_to_all(
                for_sending(scales_two[None]), "node", split_axis=1, concat_axis=0, tiled=True
            ),
        )
    )
    weight_grad = (node_sums / (node_count * local_count)).reshape(block_count, block_width)
    return (key_states, token_grad, weight_grad)


def solution(mesh):
    placed = (
        P(("node", "local"), None),
        P(),
        P("local", None),
        P("local"),
        P(("node", "local"), None),
    )
    return jax.shard_map(
        body,
        mesh=mesh,
        in_specs=placed,
        out_specs=(
            P(("node", "local"), None),
            P(("node", "local"), None),
            P(("node", "local"), None),
        ),
        check_vma=False,
    )
```

profile of v0, /device:TPU:49, one launch (start us, length us, event | category | flops | bytes accessed | tf_op | source)
XLA Modules:
  0.0 469.6 jit_solution(11482981788459198043)
XLA Ops:
  8.6 24.0 %all-gather = bf16[16,1,128]{2,1,0:T(2,128)(2,1)S(1)} all-gather(bf16[1,1,128]{2,1,0:T(2,128)(2,1)S(1)} %convert_bitcast_fusion.3), channel_id=1, replica_groups=mesh['node'=32,'local'=16] {'local'}, dimensions={0}, use_global_device_ids=true | all-gather | bytes 4352 | tf_op jit(solution)/shard_map/all_gather | solution.py:40
  32.6 3.2 copy.31
  35.8 81.3 %all-gather.3.cloned.1.call-done = bf16[2048,2048]{1,0:T(8,128)(2,1)} async-done(((bf16[128,2048]{1,0:T(8,128)(2,1)}), bf16[2048,2048]{1,0:T(8,128)(2,1)}) %all-gather.3.cloned.1.call-update) | async-done | bytes 8388624 | tf_op jit(solution)/shard_map/all_gather | solution.py:39
  117.1 8.0 %multiply_convert_fusion = bf16[2048,2048]{1,0:T(8,128)(2,1)} fusion(bf16[2048,2048]{1,0:T(8,128)(2,1)} %all-gather.3.cloned.1.call-done, f32[2048]{0:T(1024)S(1)} %bitcast.39), kind=kLoop, calls=%fused_computation.4 | loop fusion | flops 12582912 | bytes 16785408 | tf_op jit(solution)/shard_map/convert_element_type | solution.py:16
  125.1 13.9 %reshape.197 = bf16[8192,512]{1,0:T(8,128)(2,1)} reshape(bf16[2048,2048]{1,0:T(8,128)(2,1)} %multiply_convert_fusion) | data formatting | bytes 16777216 | tf_op jit(solution)/shard_map/reshape | solution.py:16
  139.0 6.0 %fusion.11 = (f32[128]{0:T(128)S(1)}, f32[128]{0:T(128)S(1)}, f32[128,8192]{0,1:T(8,128)}) fusion(bf16[128,8192]{0,1:T(8,128)(2,1)S(1)} %copy.31, f32[8192]{0:T(1024)S(1)} %copy-done.2, bf16[8192,512]{1,0:T(8,128)(2,1)} %reshape.197, bf16[128,512]{1,0:T(8,128)(2,1)S(1)} %copy-done), kind=kOutput, calls=%fused_computation.19 | convolution fusion | flops 1080033024 | bytes 14844928 | tf_op jit(solution)/shard_map/dot_general | solution.py:46
  145.1 7.0 %fusion.14 = f32[8192,512]{1,0:T(8,128)} fusion(bf16[128,512]{1,0:T(8,128)(2,1)S(1)} %copy-done, bf16[128,8192]{0,1:T(8,128)(2,1)S(1)} %copy.31, f32[8192]{0:T(1024)S(1)} %copy-done.2, f32[128]{0:T(128)S(1)} %get-tuple-element.22), kind=kOutput, calls=%fused_computation.26 | convolution fusion | flops 1077936128 | bytes 19038720 | tf_op jit(solution)/shard_map/dot_general | solution.py:55
  152.1 19.8 %reshape.198 = f32[1,32,16,4,2048]{4,3,2,1,0:T(4,128)} reshape(f32[8192,512]{1,0:T(8,128)} %fusion.14) | data formatting | bytes 33554432 | tf_op jit(solution)/shard_map/reshape | solution.py:60
  171.9 7.4 %abs_reduce_fusion = f32[32,16,4]{2,1,0:T(8,128)S(1)} fusion(f32[1,32,16,4,2048]{4,3,2,1,0:T(4,128)} %reshape.198), kind=kLoop, calls=%fused_computation.3 | loop fusion | flops 8386560 | bytes 16785408 | tf_op jit(solution)/shard_map/reduce_max | solution.py:20
  179.4 0.8 copy.34
  180.2 8.2 %all-to-all-start.1 = ((bf16[1,32,16,4]{1,3,0,2:T(4,128)(2,1)}), bf16[1,32,16,4]{1,3,0,2:T(4,128)(2,1)S(1)}, u32[]{:S(2)}, u32[]{:S(2)}) async-start(bf16[1,32,16,4]{1,3,0,2:T(4,128)(2,1)} %copy.34), calls=%async_computation.1 | async-start | bytes 32768 | tf_op jit(solution)/shard_map/all_to_all | solution.py:65
  188.4 10.4 %fusion.1 = bf16[1,32,16,4,2048]{4,3,1,0,2:T(4,128)(2,1)} fusion(f32[1,32,16,4,2048]{4,3,2,1,0:T(4,128)} %reshape.198, f32[32,16,4]{2,0,1:T(8,128)S(1)} %copy.32), kind=kLoop, calls=%fused_computation.5 | loop fusion | flops 8388608 | bytes 25174016 | tf_op jit(solution)/shard_map/convert_element_type | solution.py:21
  198.9 7.0 %all-to-all-start = ((bf16[1,32,16,4,2048]{4,3,1,0,2:T(4,128)(2,1)}), bf16[1,32,16,4,2048]{4,3,1,0,2:T(4,128)(2,1)}, u32[]{:S(2)}, u32[]{:S(2)}) async-start(bf16[1,32,16,4,2048]{4,3,1,0,2:T(4,128)(2,1)} %fusion.1), calls=%async_computation | async-start | bytes 16777216 | tf_op jit(solution)/shard_map/all_to_all | solution.py:64
  206.0 182.2 %all-to-all-done = bf16[1,32,16,4,2048]{4,3,1,0,2:T(4,128)(2,1)} async-done(((bf16[1,32,16,4,2048]{4,3,1,0,2:T(4,128)(2,1)}), bf16[1,32,16,4,2048]{4,3,1,0,2:T(4,128)(2,1)}, u32[]{:S(2)}, u32[]{:S(2)}) %all-to-all-start) | async-done | bytes 8388640 | tf_op jit(solution)/shard_map/all_to_all | solution.py:64
  388.2 8.1 %fusion = f32[32,4,2048]{2,1,0:T(4,128)S(1)} fusion(bf16[1,32,16,4,2048]{4,3,1,0,2:T(4,128)(2,1)} %all-to-all-done, f32[16,32,4]{2,1,0:T(8,128)S(1)} %copy.35), kind=kLoop, calls=%fused_computation.1 | loop fusion | flops 12320768 | bytes 9445376 | tf_op jit(solution)/shard_map/reduce_sum | solution.py:26
  396.7 0.7 copy.38
  397.5 13.5 %all-to-all-start.3 = ((bf16[1,32,1,4]{3,2,0,1:T(2,128)(2,1)}), bf16[1,32,1,4]{3,2,0,1:T(2,128)(2,1)S(1)}, u32[]{:S(2)}, u32[]{:S(2)}) async-start(bf16[1,32,1,4]{3,2,0,1:T(2,128)(2,1)} %copy.38), calls=%async_computation.3 | async-start | bytes 32768 | tf_op jit(solution)/shard_map/all_to_all | solution.py:74
  411.0 1.1 fusion.13
  412.1 12.9 %all-to-all-done.3 = bf16[1,32,1,4]{3,2,0,1:T(2,128)(2,1)S(1)} async-done(((bf16[1,32,1,4]{3,2,0,1:T(2,128)(2,1)}), bf16[1,32,1,4]{3,2,0,1:T(2,128)(2,1)S(1)}, u32[]{:S(2)}, u32[]{:S(2)}) %all-to-all-start.3) | async-done | bytes 288 | tf_op jit(solution)/shard_map/all_to_all | solution.py:74
  425.0 4.2 all-to-all-start.2
  429.2 4.5 fusion.9
  433.7 4.1 copy.41
  437.8 7.5 %convolution_convert_fusion = bf16[128,512]{1,0:T(8,128)(2,1)} fusion(bf16[8192,512]{1,0:T(8,128)(2,1)} %reshape.197, bf16[128,8192]{0,1:T(8,128)(2,1)S(1)} %copy.31, f32[8192]{0:T(1024)S(1)} %copy-done.3, f32[128]{0:T(128)S(1)} %get-tuple-element.22), kind=kOutput, calls=%fused_computation.20 | convolution fusion | flops 1078001664 | bytes 10650112 | tf_op jit(solution)/shard_map/dot_general | solution.py:45
  445.5 16.4 %all-to-all-done.2 = bf16[1,32,1,4,2048]{4,3,2,0,1:T(4,128)(2,1)S(1)} async-done(((bf16[1,32,1,4,2048]{4,3,2,0,1:T(4,128)(2,1)}), bf16[1,32,1,4,2048]{4,3,2,0,1:T(4,128)(2,1)S(1)}, u32[]{:S(2)}, u32[]{:S(2)}) %all-to-all-start.2) | async-done | bytes 524320 | tf_op jit(solution)/shard_map/all_to_all | solution.py:73
  (27 shorter events, 3.4 us)
Async XLA Ops:
  7.2 131.9 %copy-start = (bf16[128,512]{1,0:T(8,128)(2,1)S(1)}, bf16[128,512]{1,0:T(8,128)(2,1)}, u32[]{:S(2)}) copy-start(bf16[128,512]{1,0:T(8,128)(2,1)} %param.9) | copy-start | bytes 393220
  7.2 110.0 %all-gather.3.cloned.1.call-start = ((), (), s32[]{:S(2)}) async-start(), calls=%async_computation.4 | async-start | bytes 8912896 | tf_op jit(solution)/shard_map/all_gather | solution.py:39
  125.1 13.9 %copy-start.2 = (f32[8192]{0:T(1024)S(1)}, f32[8192]{0:T(1024)}, u32[]{:S(2)}) copy-start(f32[8192]{0:T(1024)} %param.6) | copy-start | bytes 98308
  180.2 18.7 %all-to-all-start.1 = ((bf16[1,32,16,4]{1,3,0,2:T(4,128)(2,1)}), bf16[1,32,16,4]{1,3,0,2:T(4,128)(2,1)S(1)}, u32[]{:S(2)}, u32[]{:S(2)}) async-start(bf16[1,32,16,4]{1,3,0,2:T(4,128)(2,1)} %copy.34), calls=%async_computation.1 | async-start | bytes 32768 | tf_op jit(solution)/shard_map/all_to_all | solution.py:65
  198.9 189.4 %all-to-all-start = ((bf16[1,32,16,4,2048]{4,3,1,0,2:T(4,128)(2,1)}), bf16[1,32,16,4,2048]{4,3,1,0,2:T(4,128)(2,1)}, u32[]{:S(2)}, u32[]{:S(2)}) async-start(bf16[1,32,16,4,2048]{4,3,1,0,2:T(4,128)(2,1)} %fusion.1), calls=%async_computation | async-start | bytes 16777216 | tf_op jit(solution)/shard_map/all_to_all | solution.py:64
  397.5 27.6 %all-to-all-start.3 = ((bf16[1,32,1,4]{3,2,0,1:T(2,128)(2,1)}), bf16[1,32,1,4]{3,2,0,1:T(2,128)(2,1)S(1)}, u32[]{:S(2)}, u32[]{:S(2)}) async-start(bf16[1,32,1,4]{3,2,0,1:T(2,128)(2,1)} %copy.38), calls=%async_computation.3 | async-start | bytes 32768 | tf_op jit(solution)/shard_map/all_to_all | solution.py:74
  425.0 36.8 %all-to-all-start.2 = ((bf16[1,32,1,4,2048]{4,3,2,0,1:T(4,128)(2,1)}), bf16[1,32,1,4,2048]{4,3,2,0,1:T(4,128)(2,1)S(1)}, u32[]{:S(2)}, u32[]{:S(2)}) async-start(bf16[1,32,1,4,2048]{4,3,2,0,1:T(4,128)(2,1)} %fusion.13), calls=%async_computation.2 | async-start | bytes 1048576 | tf_op jit(solution)/shard_map/all_to_all | solution.py:73
  433.7 4.1 copy-start.3
  433.7 29.1 %copy-start.1 = (bf16[128,512]{1,0:T(8,128)(2,1)S(1)}, bf16[128,512]{1,0:T(8,128)(2,1)}, u32[]{:S(2)}) copy-start(bf16[128,512]{1,0:T(8,128)(2,1)} %param.9) | copy-start | bytes 393220
Sparse Core Ops, SparseCore 0:
  10.1 106.9 all-gather.2
where the time goes:
time: 471 us; the launch traced here: 470 us
  waiting for transfers between devices  293 us (62%)
  local copies, waits for them, and re-layouts  43.2 us (9%)
  other arithmetic  41.5 us (9%)
  starting transfers between devices  32.8 us (7%)
  blocking collectives  24 us (5%)
  matrix products  20.5 us (4%)
  between operations  14.1 us (3%)
    all_to_all x1, waiting for transfers between devices, body(): lax.all_to_all(codes_one, 'local', split_axis=2, concat_axis=0, tiled=True)  182 us
    all_gather x1, waiting for transfers between devices, body(): lax.all_gather(weight_codes, 'local', axis=0, tiled=True)  81.3 us
    all_gather x1, blocking collectives, body(): lax.all_gather(weight_scales.astype(jnp.bfloat16), 'local', axis=0, tiled...  24 us
    reshape x1, local copies, waits for them, and re-layouts, body(): partial_grad.reshape(1, node_count, local_count, block_count, block_width)  19.8 us
    all_to_all x1, waiting for transfers between devices, body(): lax.all_to_all(codes_two[None], 'node', split_axis=1, concat_axis=0, tile...  16.4 us
    reshape x1, local copies, waits for them, and re-layouts, unpack_weight(): return dequantized.astype(jnp.bfloat16).reshape(-1, kv_width)  13.9 us
    all_to_all x1, starting transfers between devices, body(): lax.all_to_all(for_sending(scales_two[None]), 'node', split_axis=1, conca...  13.5 us
    all_to_all x1, waiting for transfers between devices, body(): lax.all_to_all(for_sending(scales_two[None]), 'node', split_axis=1, conca...  12.9 us
  transfers between devices with their start and end apart: 5, of which 4 were waited for; matrix products, arithmetic and copies ran while one was open for 7% of the time, Pallas kernels for 0%

commit v1 on v0

v1 whole, which is shorter than its diff:
```python
import jax
import jax.numpy as jnp
from jax import lax
from jax.experimental import pallas as pl
from jax.experimental.pallas import tpu as pltpu
from jax.sharding import PartitionSpec as P

EPSILON = 1e-05
MESH = pl.DeviceIdType.MESH
F32, BF16 = jnp.float32, jnp.bfloat16
TOK, D, KV = 128, 8192, 512
SHARD = 512
ORDER = (2, 1, 3, 0)
NT = (((1,), (1,)), ((), ()))
P1M, P1P, P1A, P1B = 0, 1, 2, 3
US = (0, -1, 1, 2)


def p2(u, kind):
    return 4 + 4 * US.index(u) + kind


def kernel(
    tokens, gain, codes, scales, cotangent,
    key_out, tgrad_out, wgrad_out,
    tok, kc, cod, wf, w, t, kcs, sg, tg, keyb, pf, pb, yr, sf, sb, zr, rb, zh,
    load_sem, tok_s, tok_r, kc_s, kcx_r, kcd_r, ag_s, ag_r, dd_s, dd_r, rs_s, y_r, z1_r, z2_r, out_sem,
):
    node, local = lax.axis_index("node"), lax.axis_index("local")
    x, zhi, c = node // 8, (node // 2) % 4, node % 2
    zlo, y = local // 4, local % 4
    z = zhi * 4 + zlo

    def dev(x_, y_, z_, c_):
        return (x_ * 8 + (z_ // 4) * 2 + c_, (z_ % 4) * 4 + y_)

    partner = dev(x, y, z, 1 - c)

    def at(dy=0, dz=0):
        return dev(x, (y + dy + 4) % 4, (z + dz + 16) % 16, c)

    def remote(src, dst, ssem, rsem, device):
        cp = pltpu.make_async_remote_copy(
            src_ref=src, dst_ref=dst, send_sem=ssem, recv_sem=rsem, device_id=device, device_id_type=MESH
        )
        cp.start()

    def drain(ref, sem):
        pltpu.make_async_copy(ref, ref, sem).wait()

    barrier = pltpu.get_barrier_semaphore()
    greet = [partner]
    greet += [dev((x + dx) % 4, y, z, cc) for dx in (1, 2, 3) for cc in (0, 1)]
    greet += [at(dy=e) for e in (1, 2, 3)]
    greet += [at(dz=1), at(dz=-1)]
    greet += [dev(x, y, zhi * 4 + (zlo + e) % 4, c) for e in (1, 2, 3)]
    greet += [dev(x, y, ((zhi + e) % 4) * 4 + zlo, c) for e in (1, 2, 3)]
    for who in greet:
        pl.semaphore_signal(barrier, inc=1, device_id=who, device_id_type=MESH)

    ld_cod = pltpu.make_async_copy(codes.at[pl.ds(pl.multiple_of(c * 64, 64), 64)], cod, load_sem.at[0])
    ld_tok = pltpu.make_async_copy(tokens, tok, load_sem.at[1])
    ld_kc = pltpu.make_async_copy(cotangent, kc, load_sem.at[2])
    ld_cod.start()
    ld_tok.start()
    ld_kc.start()

    slot = pl.multiple_of((x * 2 + c) * TOK, TOK)

    def chunk_cols(x_, c_, j):
        return pl.ds(pl.multiple_of(x_ * 2048 + ((zhi + ORDER[j]) % 4) * 512 + c_ * 256, 256), 256)

    for j in range(4):
        pltpu.make_async_copy(
            tokens.at[:, chunk_cols(x, c, j)], t.at[pl.ds(pl.multiple_of(j * 1024 + slot, TOK), TOK)], tok_r.at[j]
        ).start()

    ld_cod.wait()
    row = jnp.broadcast_to(scales[...], (128, 128))
    cols = jnp.transpose(row)
    wf[pl.ds(0, 128), :] = cols
    col = wf[pl.ds(pl.multiple_of(c * 64, 64), 64), :]
    for i in range(16):
        part = cod[:, i * 128:(i + 1) * 128].astype(F32) * col
        wf[pl.ds((i % 4) * 256 + i // 4, 64, stride=4), :] = part

    def piece(dy, dz, part, half=None):
        l = ((zlo + dz + 4) % 4) * 4 + (y + dy + 4) % 4
        base = l * SHARD + c * 256 + part * 128
        if half is None:
            return w.at[pl.ds(pl.multiple_of(base, 128), 128)]
        return w.at[pl.ds(pl.multiple_of(base + 64 * half, 64), 64)]

    def both(dy, dz):
        l = ((zlo + dz + 4) % 4) * 4 + (y + dy + 4) % 4
        return w.at[pl.ds(pl.multiple_of(l * SHARD + c * 256, 256), 256)]

    for i in range(4):
        both(0, 0)[:, i * 128:(i + 1) * 128] = wf[i * 256:(i + 1) * 256, :].astype(BF16)

    pl.semaphore_wait(barrier, len(greet))

    def uv(part, du, dv):
        return (du, dv) if part == 0 else (dv, du)

    def ag_send(part, du, dv, axis, step, kind, half=None):
        dy, dz = uv(part, du, dv)
        ref = piece(dy, dz, part, half)
        to = uv(part, step if axis == 0 else 0, step if axis == 1 else 0)
        remote(ref, ref, ag_s, ag_r.at[part * 20 + kind], at(*to))

    def ag_wait(part, du, dv, kind, half=None):
        dy, dz = uv(part, du, dv)
        drain(piece(dy, dz, part, half), ag_r.at[part * 20 + kind])

    def hand(part, du, dv):
        dy, dz = uv(part, du, dv)
        ref = piece(dy, dz, part)
        late = dy == 2 or dz == 2
        remote(ref, ref, dd_s, dd_r.at[1 if late else 0], partner)

    def spread(part, du):
        ag_send(part, du, 0, 1, 1, p2(du, 0))
        ag_send(part, du, 0, 1, -1, p2(du, 1))

    def relay(part, du):
        ag_wait(part, du, -1, p2(du, 0))
        ag_send(part, du, -1, 1, 1, p2(du, 2), 0)
        hand(part, du, -1)
        ag_wait(part, du, 1, p2(du, 1))
        ag_send(part, du, 1, 1, -1, p2(du, 3), 1)
        hand(part, du, 1)

    def last(part, du):
        ag_wait(part, du, 2, p2(du, 2), 0)
        ag_wait(part, du, 2, p2(du, 3), 1)
        hand(part, du, 2)

    def tok_send(j):
        for dx in (1, 3, 2):
            for cc in (0, 1):
                x_ = (x + dx) % 4
                remote(
                    tokens.at[:, chunk_cols(x_, cc, j)],
                    t.at[pl.ds(pl.multiple_of(j * 1024 + slot, TOK), TOK)],
                    tok_s, tok_r.at[j], dev(x_, y, z, cc),
                )
        remote(
            tokens.at[:, chunk_cols(x, 1 - c, j)],
            t.at[pl.ds(pl.multiple_of(j * 1024 + slot, TOK), TOK)],
            tok_s, tok_r.at[j], partner,
        )

    for part in (0, 1):
        ag_send(part, 0, 0, 0, 1, P1M)
        ag_send(part, 0, 0, 0, -1, P1P)
    tok_send(0)
    for part in (0, 1):
        spread(part, 0)
        hand(part, 0, 0)

    ld_tok.wait()

    def sq(i, acc):
        for s in range(4):
            v = tok[:, pl.ds(pl.multiple_of(i * 512 + s * 128, 128), 128)].astype(F32)
            acc = acc + v * v
        return acc

    acc = lax.fori_loop(0, 16, sq, jnp.zeros((TOK, 128), F32))
    inv = lax.rsqrt(jnp.sum(acc, axis=-1, keepdims=True) * (1.0 / D) + EPSILON)
    ld_kc.wait()
    own_kc = kcs.at[pl.ds(slot, TOK)]
    own_kc[...] = (kc[...].astype(F32) * inv).astype(BF16)
    for dx in (1, 3, 2):
        remote(own_kc, own_kc, kc_s, kcx_r, dev((x + dx) % 4, y, z, c))
    remote(own_kc, own_kc, kc_s, kcd_r, partner)
    for j in (1, 2, 3):
        tok_send(j)

    def shard(l, carry):
        keys, inner = carry
        cs = pl.ds(pl.multiple_of(l * SHARD, SHARD), SHARD)
        wl = w[cs, :]
        tf = tok[:, cs].astype(F32)
        g = gain[:, cs]
        normed = (tf * inv * g).astype(BF16)
        keys = keys + jnp.dot(normed, wl, preferred_element_type=F32)
        s = lax.dot_general(kc[...], wl, NT, preferred_element_type=F32) * g
        sg[:, cs] = s
        pr = tf * s
        inner = inner + (pr[:, :128] + pr[:, 128:256]) + (pr[:, 256:384] + pr[:, 384:])
        return keys, inner

    def l_of(dy, dz):
        return ((zlo + dz + 4) % 4) * 4 + (y + dy + 4) % 4

    def chunk_matmul(j):
        drain(t.at[pl.ds(j * 1024, 1024)], tok_r.at[j])
        base = x * 2048 + ((zhi + ORDER[j]) % 4) * 512 + c * 256
        for b in range(2):
            a = t[j * 1024:(j + 1) * 1024, b * 128:(b + 1) * 128]
            r = lax.dot_general(a, kcs[...], (((0,), (0,)), ((), ())), preferred_element_type=F32)
            g = gain[:, pl.ds(pl.multiple_of(base + b * 128, 128), 128)]
            gcol = jnp.transpose(jnp.broadcast_to(g, (128, 128)))
            r = jnp.concatenate([r[:, i * 128:(i + 1) * 128] * gcol for i in range(4)], axis=1)
            for zl in range(2):
                for yy in range(4):
                    piece_ = r[(zl * 4 + yy) * 16:(zl * 4 + yy + 1) * 16]
                    o = yy * 64 + (2 * b + zl) * 16
                    pf[o:o + 16, :] = piece_
                    pb[j * 256 + o:j * 256 + o + 16, :] = piece_.astype(BF16)
        for e in (1, 3, 2):
            y_ = (y + e) % 4
            remote(
                pb.at[pl.ds(pl.multiple_of(j * 256 + y_ * 64, 64), 64)],
                yr.at[pl.ds(j * 192 + (e - 1) * 64, 64)],
                rs_s, y_r.at[j], dev(x, y_, z, c),
            )
        sf[j * 64:(j + 1) * 64, :] = pf[pl.ds(pl.multiple_of(y * 64, 64), 64), :]

    def y_sum(j):
        drain(yr.at[pl.ds(j * 192, 192)], y_r.at[j])
        s = sf[j * 64:(j + 1) * 64, :]
        for e in range(3):
            s = s + yr[j * 192 + e * 64:j * 192 + (e + 1) * 64, :].astype(F32)
        sf[j * 64:(j + 1) * 64, :] = s
        sb[j * 64:(j + 1) * 64, :] = s.astype(BF16)
        for e in (1, 3, 2):
            zl = (zlo + e) % 4
            remote(
                sb.at[pl.ds(pl.multiple_of(j * 64 + zl * 16, 16), 16)],
                zr.at[pl.ds(j * 48 + (e - 1) * 16, 16)],
                rs_s, z1_r.at[j], dev(x, y, zhi * 4 + zl, c),
            )

    def z_sum(j):
        drain(zr.at[pl.ds(j * 48, 48)], z1_r.at[j])
        s = sf[pl.ds(pl.multiple_of(j * 64 + zlo * 16, 16), 16), :]
        for e in range(3):
            s = s + zr[j * 48 + e * 16:j * 48 + (e + 1) * 16, :].astype(F32)
        return s

    def z_far(j):
        rb[j * 16:(j + 1) * 16, :] = z_sum(j).astype(BF16)
        remote(
            rb.at[pl.ds(j * 16, 16)], zh.at[pl.ds(j * 16, 16)], rs_s, z2_r,
            dev(x, y, ((zhi + ORDER[j]) % 4) * 4 + zlo, c),
        )

    for part in (0, 1):
        ag_wait(part, -1, 0, P1M)
        ag_send(part, -1, 0, 0, 1, P1A, 0)
        ag_wait(part, 1, 0, P1P)
        ag_send(part, 1, 0, 0, -1, P1B, 1)
    for part in (0, 1):
        for du in (-1, 1):
            spread(part, du)
            hand(part, du, 0)
    for part in (0, 1):
        relay(part, 0)
    for part in (0, 1):
        ag_wait(part, 2, 0, P1A, 0)
        ag_wait(part, 2, 0, P1B, 1)
        spread(part, 2)
        hand(part, 2, 0)
    for part in (0, 1):
        relay(part, -1)
    drain(kcs.at[pl.ds(0, 384)], kcx_r)
    for dx in (1, 2, 3):
        ref = kcs.at[pl.ds(pl.multiple_of((((x + dx) % 4) * 2 + c) * TOK, TOK), TOK)]
        remote(ref, ref, kc_s, kcd_r, partner)
    for part in (0, 1):
        relay(part, 1)
    drain(kcs.at[pl.ds(0, 512)], kcd_r)
    chunk_matmul(0)
    for part in (0, 1):
        relay(part, 2)
    y_sum(0)
    drain(w.at[pl.ds(0, 9 * 256)], dd_r.at[0])
    carry = (jnp.zeros((TOK, KV), F32), jnp.zeros((TOK, 128), F32))
    carry = lax.fori_loop(0, 9, lambda i, cr: shard(l_of(i % 3 - 1, i // 3 - 1), cr), carry)
    z_far(0)
    chunk_matmul(1)
    for part in (0, 1):
        for du in US:
            last(part, du)
    y_sum(1)
    drain(w.at[pl.ds(0, 7 * 256)], dd_r.at[1])
    carry = lax.fori_loop(0, 4, lambda i, cr: shard(l_of(2, i - 1), cr), carry)
    z_far(1)
    chunk_matmul(2)
    carry = lax.fori_loop(0, 3, lambda i, cr: shard(l_of(i - 1, 2), cr), carry)
    keys, inner = carry
    keyb[...] = keys.astype(BF16)
    key_copy = pltpu.make_async_copy(keyb, key_out, out_sem.at[0])
    key_copy.start()
    y_sum(2)
    mean = jnp.sum(inner, axis=-1, keepdims=True) * (1.0 / D)
    coef = inv * inv * mean
    z_far(2)
    chunk_matmul(3)

    def final(i, _):
        cs = pl.ds(pl.multiple_of(i * 512, 512), 512)
        tg[:, cs] = (inv * (sg[:, cs] - tok[:, cs].astype(F32) * coef)).astype(BF16)
        return 0

    lax.fori_loop(0, 16, final, 0)
    tg_copy = pltpu.make_async_copy(tg, tgrad_out, out_sem.at[1])
    tg_copy.start()
    y_sum(3)
    s = z_sum(3)
    drain(zh, z2_r)
    for j in range(3):
        s = s + zh[j * 16:(j + 1) * 16, :].astype(F32)
    s = s * (1.0 / 512)
    for i in range(4):
        wf[i * 16:(i + 1) * 16, :] = s[:, i * 128:(i + 1) * 128]
    for i in range(4):
        for q in range(4):
            wgrad_out[:, i * KV + q * 128:i * KV + (q + 1) * 128] = wf[pl.ds(q * 16 + i, 4, stride=4), :]

    key_copy.wait()
    tg_copy.wait()
    drain(t.at[pl.ds(0, 3584)], tok_s)
    drain(kcs.at[pl.ds(0, 896)], kc_s)
    drain(w.at[pl.ds(0, 3840)], ag_s)
    drain(w.at[pl.ds(0, 4096)], dd_s)
    drain(pb.at[pl.ds(0, 1008)], rs_s)


def body(tokens, gain, codes, scales, cotangent):
    dma = pltpu.SemaphoreType.DMA
    any_ = pl.BlockSpec(memory_space=pl.ANY)
    vmem = pl.BlockSpec(memory_space=pltpu.VMEM)
    return pl.pallas_call(
        kernel,
        out_shape=(
            jax.ShapeDtypeStruct((TOK, KV), BF16),
            jax.ShapeDtypeStruct((TOK, D), BF16),
            jax.ShapeDtypeStruct((4, 2048), F32),
        ),
        in_specs=[any_, vmem, any_, vmem, any_],
        out_specs=(any_, any_, vmem),
        scratch_shapes=[
            pltpu.VMEM((TOK, D), BF16),
            pltpu.VMEM((TOK, KV), BF16),
            pltpu.VMEM((64, 2048), BF16),
            pltpu.VMEM((1024, 128), F32),
            pltpu.VMEM((D, KV), BF16),
            pltpu.VMEM((4096, 256), BF16),
            pltpu.VMEM((1024, KV), BF16),
            pltpu.VMEM((TOK, D), F32),
            pltpu.VMEM((TOK, D), BF16),
            pltpu.VMEM((TOK, KV), BF16),
            pltpu.VMEM((256, KV), F32),
            pltpu.VMEM((1024, KV), BF16),
            pltpu.VMEM((768, KV), BF16),
            pltpu.VMEM((256, KV), F32),
            pltpu.VMEM((256, KV), BF16),
            pltpu.VMEM((192, KV), BF16),
            pltpu.VMEM((48, KV), BF16),
            pltpu.VMEM((48, KV), BF16),
            dma((3,)),
            dma, dma((4,)),
            dma, dma, dma,
            dma, dma((40,)),
            dma, dma((2,)),
            dma, dma((4,)), dma((4,)), dma,
            dma((2,)),
        ],
        compiler_params=pltpu.CompilerParams(
            collective_id=0, has_side_effects=True, vmem_limit_bytes=48 * 1024 * 1024
        ),
        name="key_projection",
    )(tokens, gain.reshape(1, D), codes, scales.reshape(1, 128), cotangent)


def solution(mesh):
    rows = P(("node", "local"), None)
    return jax.shard_map(
        body,
        mesh=mesh,
        in_specs=(rows, P(), P("local", None), P("local"), rows),
        out_specs=(rows, rows, rows),
        check_vma=False,
    )
```

time: 471 us -> 80.6 us (0.17)
  the two profiles are of different devices: /device:TPU:49 before, /device:TPU:4 now
where the time goes in v1:
time: 80.6 us; the launch traced here: 80.4 us
  Pallas kernels  72.2 us (90%)
  local copies, waits for them, and re-layouts  7.53 us (9%)
    pallas_call x1, Pallas kernels, body(): pl.pallas_call(kernel, out_shape=(jax.ShapeDtypeStruct((TOK, KV), BF16),...  72.2 us
    unnamed x13, local copies, waits for them, and re-layouts  7.53 us

profile of v1, /device:TPU:4, one launch (start us, length us, event | category | flops | bytes accessed | tf_op | source)
XLA Modules:
  0.0 80.4 jit_solution(8878214964233893610)
XLA Ops:
  0.6 0.0 copy-start
  0.6 1.6 %copy-done = bf16[128,8192]{1,0:T(8,128)(2,1)S(1)} copy-done((bf16[128,8192]{1,0:T(8,128)(2,1)S(1)}, bf16[128,8192]{1,0:T(8,128)(2,1)}, u32[]{:S(2)}) %copy-start) | copy-done | bytes 2097176
  2.2 0.0 copy-start.1
  2.2 1.0 %copy-done.1 = bf16[128,2048]{1,0:T(8,128)(2,1)S(1)} copy-done((bf16[128,2048]{1,0:T(8,128)(2,1)S(1)}, bf16[128,2048]{1,0:T(8,128)(2,1)}, u32[]{:S(2)}) %copy-start.1) | copy-done | bytes 524312
  3.3 0.0 copy-start.2
  3.3 0.9 %copy-done.2 = bf16[128,512]{1,0:T(8,128)(2,1)S(1)} copy-done((bf16[128,512]{1,0:T(8,128)(2,1)S(1)}, bf16[128,512]{1,0:T(8,128)(2,1)}, u32[]{:S(2)}) %copy-start.2) | copy-done | bytes 131096
  4.2 0.0 copy-start.3
  4.2 0.8 copy-done.3
  4.9 0.0 copy-start.4
  4.9 0.7 copy-done.4
  5.6 72.2 %key_projection.1 = (bf16[128,512]{1,0:T(8,128)(2,1)S(1)}, bf16[128,8192]{1,0:T(8,128)(2,1)S(1)}, f32[4,2048]{1,0:T(4,128)S(1)}) custom-call(bf16[128,8192]{1,0:T(8,128)(2,1)S(1)} %copy-done, f32[1,8192]{1,0:T(1,128)S(1)} %bitcast.2, bf16[128,2048]{1,0:T(8,128)(2,1)S(1)} %copy-done.1, f32[1,128]{1,0:T(1,128)S(1)} %bitcast.3, bf16[128,512]{1,0:T(8,128)(2,1)S(1)} %copy-done.2), custom_call_target="tpu_custom_call" | custom-call | tf_op jit(solution)/shard_map/key_projection/pallas_call | solution.py:337
  77.8 0.7 copy.11
  78.4 1.3 %copy.12 = bf16[128,8192]{1,0:T(8,128)(2,1)} copy(bf16[128,8192]{1,0:T(8,128)(2,1)S(1)} %get-tuple-element.7) | data formatting | bytes 4194304
  79.7 0.6 copy.13
Async XLA Ops:
  0.6 1.6 %copy-start = (bf16[128,8192]{1,0:T(8,128)(2,1)S(1)}, bf16[128,8192]{1,0:T(8,128)(2,1)}, u32[]{:S(2)}) copy-start(bf16[128,8192]{1,0:T(8,128)(2,1)} %tokens.1) | copy-start | bytes 6291460
  2.2 1.0 %copy-start.1 = (bf16[128,2048]{1,0:T(8,128)(2,1)S(1)}, bf16[128,2048]{1,0:T(8,128)(2,1)}, u32[]{:S(2)}) copy-start(bf16[128,2048]{1,0:T(8,128)(2,1)} %codes.1) | copy-start | bytes 1572868
  3.3 0.9 %copy-start.2 = (bf16[128,512]{1,0:T(8,128)(2,1)S(1)}, bf16[128,512]{1,0:T(8,128)(2,1)}, u32[]{:S(2)}) copy-start(bf16[128,512]{1,0:T(8,128)(2,1)} %cotangent.1) | copy-start | bytes 393220
  4.2 0.8 copy-start.3
  4.9 0.7 copy-start.4

commit v2 on v1

--- a/solution.py
+++ b/solution.py
@@ -12,8 +12,14 @@
 SHARD = 512
 ORDER = (2, 1, 3, 0)
 NT = (((1,), (1,)), ((), ()))
+STEPS = (
+    "start", "first", "kc_relay", "first_spread", "relay0", "second", "relay-", "kc_last", "relay+", "kc_all",
+    "m0", "relay2", "y0", "m1", "early", "z0", "y1", "m2", "z1", "y2", "last0", "last-", "last+",
+    "m3", "z2", "last2", "y3", "late", "token_grad", "weight_grad",
+)
 P1M, P1P, P1A, P1B = 0, 1, 2, 3
 US = (0, -1, 1, 2)
+ROWS, START, CUT = (144, 112), (0, 144), (80, 48)
 
 
 def p2(u, kind):
@@ -21,9 +27,9 @@
 
 
 def kernel(
-    tokens, gain, codes, scales, cotangent,
+    tokens, gain_in, codes, scales_in, cotangent,
     key_out, tgrad_out, wgrad_out,
-    tok, kc, cod, wf, w, t, kcs, sg, tg, keyb, pf, pb, yr, sf, sb, zr, rb, zh,
+    gain, scales, tok, kc, cod, wf, w, t, kcs, sg, tg, keyb, pf, pb, yr, sf, sb, zr, rb, zh,
     load_sem, tok_s, tok_r, kc_s, kcx_r, kcd_r, ag_s, ag_r, dd_s, dd_r, rs_s, y_r, z1_r, z2_r, out_sem,
 ):
     node, local = lax.axis_index("node"), lax.axis_index("local")
@@ -54,16 +60,17 @@
     greet += [at(dy=e) for e in (1, 2, 3)]
     greet += [at(dz=1), at(dz=-1)]
     greet += [dev(x, y, zhi * 4 + (zlo + e) % 4, c) for e in (1, 2, 3)]
-    greet += [dev(x, y, ((zhi + e) % 4) * 4 + zlo, c) for e in (1, 2, 3)]
+    greet += [at(dz=4), at(dz=-4)]
     for who in greet:
         pl.semaphore_signal(barrier, inc=1, device_id=who, device_id_type=MESH)
 
     ld_cod = pltpu.make_async_copy(codes.at[pl.ds(pl.multiple_of(c * 64, 64), 64)], cod, load_sem.at[0])
     ld_tok = pltpu.make_async_copy(tokens, tok, load_sem.at[1])
     ld_kc = pltpu.make_async_copy(cotangent, kc, load_sem.at[2])
-    ld_cod.start()
-    ld_tok.start()
-    ld_kc.start()
+    ld_sc = pltpu.make_async_copy(scales_in, scales, load_sem.at[3])
+    ld_gain = pltpu.make_async_copy(gain_in, gain, load_sem.at[4])
+    for ld in (ld_tok, ld_kc, ld_sc, ld_cod, ld_gain):
+        ld.start()
 
     slot = pl.multiple_of((x * 2 + c) * TOK, TOK)
 
@@ -75,6 +82,7 @@
             tokens.at[:, chunk_cols(x, c, j)], t.at[pl.ds(pl.multiple_of(j * 1024 + slot, TOK), TOK)], tok_r.at[j]
         ).start()
 
+    ld_sc.wait()
     ld_cod.wait()
     row = jnp.broadcast_to(scales[...], (128, 128))
     cols = jnp.transpose(row)
@@ -86,10 +94,13 @@
 
     def piece(dy, dz, part, half=None):
         l = ((zlo + dz + 4) % 4) * 4 + (y + dy + 4) % 4
-        base = l * SHARD + c * 256 + part * 128
-        if half is None:
-            return w.at[pl.ds(pl.multiple_of(base, 128), 128)]
-        return w.at[pl.ds(pl.multiple_of(base + 64 * half, 64), 64)]
+        base = l * SHARD + c * 256 + START[part]
+        rows = ROWS[part]
+        if half == 0:
+            rows = CUT[part]
+        elif half == 1:
+            base, rows = base + CUT[part], rows - CUT[part]
+        return w.at[pl.ds(pl.multiple_of(base, 16), rows)]
 
     def both(dy, dz):
         l = ((zlo + dz + 4) % 4) * 4 + (y + dy + 4) % 4
@@ -97,8 +108,6 @@
 
     for i in range(4):
         both(0, 0)[:, i * 128:(i + 1) * 128] = wf[i * 256:(i + 1) * 256, :].astype(BF16)
-
-    pl.semaphore_wait(barrier, len(greet))
 
     def uv(part, du, dv):
         return (du, dv) if part == 0 else (dv, du)
@@ -151,14 +160,6 @@
             tok_s, tok_r.at[j], partner,
         )
 
-    for part in (0, 1):
-        ag_send(part, 0, 0, 0, 1, P1M)
-        ag_send(part, 0, 0, 0, -1, P1P)
-    tok_send(0)
-    for part in (0, 1):
-        spread(part, 0)
-        hand(part, 0, 0)
-
     ld_tok.wait()
 
     def sq(i, acc):
@@ -172,11 +173,20 @@
     ld_kc.wait()
     own_kc = kcs.at[pl.ds(slot, TOK)]
     own_kc[...] = (kc[...].astype(F32) * inv).astype(BF16)
-    for dx in (1, 3, 2):
-        remote(own_kc, own_kc, kc_s, kcx_r, dev((x + dx) % 4, y, z, c))
-    remote(own_kc, own_kc, kc_s, kcd_r, partner)
-    for j in (1, 2, 3):
-        tok_send(j)
+
+    def kc_of(dx, half=None):
+        base = (((x + dx + 4) % 4) * 2 + c) * TOK
+        if half is None:
+            return kcs.at[pl.ds(pl.multiple_of(base, TOK), TOK)]
+        return kcs.at[pl.ds(pl.multiple_of(base + half * 64, 64), 64)]
+
+    def kc_send(dx, step, kind, half=None):
+        ref = kc_of(dx, half)
+        remote(ref, ref, kc_s, kcx_r.at[kind], dev((x + step + 4) % 4, y, z, c))
+
+    def kc_hand(dx):
+        ref = kc_of(dx)
+        remote(ref, ref, kc_s, kcd_r, partner)
 
     def shard(l, carry):
         keys, inner = carry
@@ -210,14 +220,14 @@
                     o = yy * 64 + (2 * b + zl) * 16
                     pf[o:o + 16, :] = piece_
                     pb[j * 256 + o:j * 256 + o + 16, :] = piece_.astype(BF16)
-        for e in (1, 3, 2):
+        sf[j * 64:(j + 1) * 64, :] = pf[pl.ds(pl.multiple_of(y * 64, 64), 64), :]
+        for e in (2, 1, 3):
             y_ = (y + e) % 4
             remote(
                 pb.at[pl.ds(pl.multiple_of(j * 256 + y_ * 64, 64), 64)],
                 yr.at[pl.ds(j * 192 + (e - 1) * 64, 64)],
                 rs_s, y_r.at[j], dev(x, y_, z, c),
             )
-        sf[j * 64:(j + 1) * 64, :] = pf[pl.ds(pl.multiple_of(y * 64, 64), 64), :]
 
     def y_sum(j):
         drain(yr.at[pl.ds(j * 192, 192)], y_r.at[j])
@@ -226,7 +236,7 @@
             s = s + yr[j * 192 + e * 64:j * 192 + (e + 1) * 64, :].astype(F32)
         sf[j * 64:(j + 1) * 64, :] = s
         sb[j * 64:(j + 1) * 64, :] = s.astype(BF16)
-        for e in (1, 3, 2):
+        for e in (2, 1, 3):
             zl = (zlo + e) % 4
             remote(
                 sb.at[pl.ds(pl.multiple_of(j * 64 + zl * 16, 16), 16)],
@@ -242,84 +252,127 @@
         return s
 
     def z_far(j):
-        rb[j * 16:(j + 1) * 16, :] = z_sum(j).astype(BF16)
+        s = z_sum(j)
+        if j == 1:
+            drain(zh.at[pl.ds(0, 16)], z2_r.at[0])
+            s = s + zh[0:16, :].astype(F32)
+        rb[j * 16:(j + 1) * 16, :] = s.astype(BF16)
         remote(
-            rb.at[pl.ds(j * 16, 16)], zh.at[pl.ds(j * 16, 16)], rs_s, z2_r,
-            dev(x, y, ((zhi + ORDER[j]) % 4) * 4 + zlo, c),
+            rb.at[pl.ds(j * 16, 16)], zh.at[pl.ds(j * 16, 16)], rs_s, z2_r.at[j], at(dz=-4 if j == 2 else 4)
         )
 
-    for part in (0, 1):
+    state = {"keys": jnp.zeros((TOK, KV), F32), "inner": jnp.zeros((TOK, 128), F32)}
+
+    def start():
+        pl.semaphore_wait(barrier, len(greet))
+        kc_send(0, 1, 0)
+        kc_send(0, -1, 1)
+        tok_send(0)
+        for part in (0, 1):
+            ag_send(part, 0, 0, 0, 1, P1M)
+            ag_send(part, 0, 0, 0, -1, P1P)
+        for part in (0, 1):
+            spread(part, 0)
+            hand(part, 0, 0)
+        kc_hand(0)
+        ld_gain.wait()
+
+    def kc_relay():
+        drain(kc_of(-1), kcx_r.at[0])
+        kc_send(-1, 1, 2, 0)
+        drain(kc_of(1), kcx_r.at[1])
+        kc_send(1, -1, 3, 1)
+        for j in (1, 2, 3):
+            tok_send(j)
+        kc_hand(-1)
+        kc_hand(1)
+
+    def kc_last():
+        drain(kc_of(2, 0), kcx_r.at[2])
+        drain(kc_of(2, 1), kcx_r.at[3])
+        kc_hand(2)
+
+    def first(part):
         ag_wait(part, -1, 0, P1M)
         ag_send(part, -1, 0, 0, 1, P1A, 0)
         ag_wait(part, 1, 0, P1P)
         ag_send(part, 1, 0, 0, -1, P1B, 1)
-    for part in (0, 1):
+
+    def first_spread(part):
         for du in (-1, 1):
             spread(part, du)
             hand(part, du, 0)
-    for part in (0, 1):
-        relay(part, 0)
-    for part in (0, 1):
+
+    def second(part):
         ag_wait(part, 2, 0, P1A, 0)
         ag_wait(part, 2, 0, P1B, 1)
         spread(part, 2)
         hand(part, 2, 0)
-    for part in (0, 1):
-        relay(part, -1)
-    drain(kcs.at[pl.ds(0, 384)], kcx_r)
-    for dx in (1, 2, 3):
-        ref = kcs.at[pl.ds(pl.multiple_of((((x + dx) % 4) * 2 + c) * TOK, TOK), TOK)]
-        remote(ref, ref, kc_s, kcd_r, partner)
-    for part in (0, 1):
-        relay(part, 1)
-    drain(kcs.at[pl.ds(0, 512)], kcd_r)
-    chunk_matmul(0)
-    for part in (0, 1):
-        relay(part, 2)
-    y_sum(0)
-    drain(w.at[pl.ds(0, 9 * 256)], dd_r.at[0])
-    carry = (jnp.zeros((TOK, KV), F32), jnp.zeros((TOK, 128), F32))
-    carry = lax.fori_loop(0, 9, lambda i, cr: shard(l_of(i % 3 - 1, i // 3 - 1), cr), carry)
-    z_far(0)
-    chunk_matmul(1)
-    for part in (0, 1):
-        for du in US:
-            last(part, du)
-    y_sum(1)
-    drain(w.at[pl.ds(0, 7 * 256)], dd_r.at[1])
-    carry = lax.fori_loop(0, 4, lambda i, cr: shard(l_of(2, i - 1), cr), carry)
-    z_far(1)
-    chunk_matmul(2)
-    carry = lax.fori_loop(0, 3, lambda i, cr: shard(l_of(i - 1, 2), cr), carry)
-    keys, inner = carry
-    keyb[...] = keys.astype(BF16)
+
+    def shards(count, index):
+        state["keys"], state["inner"] = lax.fori_loop(
+            0, count, lambda i, cr: shard(l_of(*index(i)), cr), (state["keys"], state["inner"])
+        )
+
+    def early_shards():
+        drain(w.at[pl.ds(0, 9 * 256)], dd_r.at[0])
+        shards(9, lambda i: (i % 3 - 1, i // 3 - 1))
+
+    def late_shards():
+        drain(w.at[pl.ds(0, 7 * 256)], dd_r.at[1])
+        shards(4, lambda i: (2, i - 1))
+        shards(3, lambda i: (i - 1, 2))
+
     key_copy = pltpu.make_async_copy(keyb, key_out, out_sem.at[0])
-    key_copy.start()
-    y_sum(2)
-    mean = jnp.sum(inner, axis=-1, keepdims=True) * (1.0 / D)
-    coef = inv * inv * mean
-    z_far(2)
-    chunk_matmul(3)
-
-    def final(i, _):
-        cs = pl.ds(pl.multiple_of(i * 512, 512), 512)
-        tg[:, cs] = (inv * (sg[:, cs] - tok[:, cs].astype(F32) * coef)).astype(BF16)
-        return 0
-
-    lax.fori_loop(0, 16, final, 0)
     tg_copy = pltpu.make_async_copy(tg, tgrad_out, out_sem.at[1])
-    tg_copy.start()
-    y_sum(3)
-    s = z_sum(3)
-    drain(zh, z2_r)
-    for j in range(3):
-        s = s + zh[j * 16:(j + 1) * 16, :].astype(F32)
-    s = s * (1.0 / 512)
-    for i in range(4):
-        wf[i * 16:(i + 1) * 16, :] = s[:, i * 128:(i + 1) * 128]
-    for i in range(4):
-        for q in range(4):
-            wgrad_out[:, i * KV + q * 128:i * KV + (q + 1) * 128] = wf[pl.ds(q * 16 + i, 4, stride=4), :]
+
+    def token_grad():
+        keyb[...] = state["keys"].astype(BF16)
+        key_copy.start()
+        mean = jnp.sum(state["inner"], axis=-1, keepdims=True) * (1.0 / D)
+        coef = inv * inv * mean
+
+        def final(i, _):
+            cs = pl.ds(pl.multiple_of(i * 512, 512), 512)
+            tg[:, cs] = (inv * (sg[:, cs] - tok[:, cs].astype(F32) * coef)).astype(BF16)
+            return 0
+
+        lax.fori_loop(0, 16, final, 0)
+        tg_copy.start()
+
+    def weight_grad():
+        s = z_sum(3)
+        for j in (1, 2):
+            drain(zh.at[pl.ds(j * 16, 16)], z2_r.at[j])
+            s = s + zh[j * 16:(j + 1) * 16, :].astype(F32)
+        s = s * (1.0 / 512)
+        for i in range(4):
+            wf[i * 16:(i + 1) * 16, :] = s[:, i * 128:(i + 1) * 128]
+        for i in range(4):
+            for q in range(4):
+                wgrad_out[:, i * KV + q * 128:i * KV + (q + 1) * 128] = wf[pl.ds(q * 16 + i, 4, stride=4), :]
+
+    def on_parts(step, *args):
+        for part in (0, 1):
+            step(part, *args)
+
+    steps = {
+        "start": start, "kc_relay": kc_relay, "kc_last": kc_last,
+        "kc_all": lambda: drain(kcs.at[pl.ds(0, 512)], kcd_r),
+        "first": lambda: on_parts(first), "first_spread": lambda: on_parts(first_spread),
+        "second": lambda: on_parts(second),
+        "relay0": lambda: on_parts(relay, 0), "relay-": lambda: on_parts(relay, -1),
+        "relay+": lambda: on_parts(relay, 1), "relay2": lambda: on_parts(relay, 2),
+        "last0": lambda: on_parts(last, 0), "last-": lambda: on_parts(last, -1),
+        "last+": lambda: on_parts(last, 1), "last2": lambda: on_parts(last, 2),
+        "early": early_shards, "late": late_shards, "token_grad": token_grad, "weight_grad": weight_grad,
+    }
+    for j in range(4):
+        steps[f"m{j}"] = lambda j=j: chunk_matmul(j)
+        steps[f"y{j}"] = lambda j=j: y_sum(j)
+        steps[f"z{j}"] = lambda j=j: z_far(j)
+    for step in STEPS:
+        steps[step]()
 
     key_copy.wait()
     tg_copy.wait()
@@ -330,20 +383,39 @@
     drain(pb.at[pl.ds(0, 1008)], rs_s)
 
 
+def hand_over(keys, tgrad, wgrad, keys_out, tgrad_out, wgrad_out, kv, tv, wv, sem_in, sem_out):
+    parts = [(keys, kv, keys_out), (wgrad, wv, wgrad_out)]
+    for i in range(4):
+        rows = pl.ds(i * 32, 32)
+        parts.append((tgrad.at[rows], tv.at[rows], tgrad_out.at[rows]))
+    loads = [pltpu.make_async_copy(src, mid, sem_in.at[i]) for i, (src, mid, _) in enumerate(parts)]
+    stores = [pltpu.make_async_copy(mid, dst, sem_out.at[i]) for i, (_, mid, dst) in enumerate(parts)]
+    for load in loads:
+        load.start()
+    for load, store in zip(loads, stores):
+        load.wait()
+        store.start()
+    for store in stores:
+        store.wait()
+
+
 def body(tokens, gain, codes, scales, cotangent):
     dma = pltpu.SemaphoreType.DMA
-    any_ = pl.BlockSpec(memory_space=pl.ANY)
+    hbm = pl.BlockSpec(memory_space=pltpu.HBM)
     vmem = pl.BlockSpec(memory_space=pltpu.VMEM)
-    return pl.pallas_call(
+    outs = (
+        jax.ShapeDtypeStruct((TOK, KV), BF16),
+        jax.ShapeDtypeStruct((TOK, D), BF16),
+        jax.ShapeDtypeStruct((4, 2048), F32),
+    )
+    results = pl.pallas_call(
         kernel,
-        out_shape=(
-            jax.ShapeDtypeStruct((TOK, KV), BF16),
-            jax.ShapeDtypeStruct((TOK, D), BF16),
-            jax.ShapeDtypeStruct((4, 2048), F32),
-        ),
-        in_specs=[any_, vmem, any_, vmem, any_],
-        out_specs=(any_, any_, vmem),
+        out_shape=outs,
+        in_specs=[hbm] * 5,
+        out_specs=(hbm, hbm, vmem),
         scratch_shapes=[
+            pltpu.VMEM((1, D), F32),
+            pltpu.VMEM((1, 128), F32),
             pltpu.VMEM((TOK, D), BF16),
             pltpu.VMEM((TOK, KV), BF16),
             pltpu.VMEM((64, 2048), BF16),
@@ -362,19 +434,34 @@
             pltpu.VMEM((192, KV), BF16),
             pltpu.VMEM((48, KV), BF16),
             pltpu.VMEM((48, KV), BF16),
-            dma((3,)),
+            dma((5,)),
             dma, dma((4,)),
-            dma, dma, dma,
+            dma, dma((4,)), dma,
             dma, dma((40,)),
             dma, dma((2,)),
-            dma, dma((4,)), dma((4,)), dma,
+            dma, dma((4,)), dma((4,)), dma((3,)),
             dma((2,)),
         ],
         compiler_params=pltpu.CompilerParams(
-            collective_id=0, has_side_effects=True, vmem_limit_bytes=48 * 1024 * 1024
+            collective_id=0, has_side_effects=True, vmem_limit_bytes=62 * 1024 * 1024
         ),
         name="key_projection",
     )(tokens, gain.reshape(1, D), codes, scales.reshape(1, 128), cotangent)
+    return pl.pallas_call(
+        hand_over,
+        out_shape=outs,
+        in_specs=[hbm] * 3,
+        out_specs=(hbm,) * 3,
+        scratch_shapes=[
+            pltpu.VMEM((TOK, KV), BF16),
+            pltpu.VMEM((TOK, D), BF16),
+            pltpu.VMEM((4, 2048), F32),
+            dma((6,)),
+            dma((6,)),
+        ],
+        compiler_params=pltpu.CompilerParams(vmem_limit_bytes=62 * 1024 * 1024),
+        name="hand_over",
+    )(*results)
 
 
 def solution(mesh):

time: 80.6 us -> 62.8 us (0.78)
  the two profiles are of different devices: /device:TPU:4 before, /device:TPU:1 now
where the time goes in v2:
time: 62.8 us; the launch traced here: 62.7 us
  Pallas kernels  62 us (99%)
  between operations  0.64 us (1%)
    pallas_call x1, Pallas kernels, body(): pl.pallas_call(kernel, out_shape=outs, in_specs=[hbm] * 5, out_specs=(hbm...  59.5 us
    pallas_call x1, Pallas kernels, body(): pl.pallas_call(hand_over, out_shape=outs, in_specs=[hbm] * 3, out_specs=(...  2.55 us

profile of v2, /device:TPU:1, one launch (start us, length us, event | category | flops | bytes accessed | tf_op | source)
XLA Modules:
  0.0 62.7 jit_solution(13862799599292275031)
XLA Ops:
  0.6 59.5 %key_projection.1 = (bf16[128,512]{1,0:T(8,128)(2,1)}, bf16[128,8192]{1,0:T(8,128)(2,1)}, f32[4,2048]{1,0:T(4,128)}) custom-call(bf16[128,8192]{1,0:T(8,128)(2,1)} %tokens.1, f32[1,8192]{1,0:T(1,128)} %bitcast.2, bf16[128,2048]{1,0:T(8,128)(2,1)} %codes.1, f32[1,128]{1,0:T(1,128)} %bitcast.3, bf16[128,512]{1,0:T(8,128)(2,1)} %cotangent.1), custom_call_target="tpu_custom_call" | custom-call | tf_op jit(solution)/shard_map/key_projection/pallas_call | solution.py:411
  60.1 2.6 %hand_over.1 = (bf16[128,512]{1,0:T(8,128)(2,1)}, bf16[128,8192]{1,0:T(8,128)(2,1)}, f32[4,2048]{1,0:T(4,128)}) custom-call(bf16[128,512]{1,0:T(8,128)(2,1)} %get-tuple-element.6.keys, bf16[128,8192]{1,0:T(8,128)(2,1)} %get-tuple-element.7.tgrad, f32[4,2048]{1,0:T(4,128)} %get-tuple-element.8.wgrad), custom_call_target="tpu_custom_call" | custom-call | tf_op jit(solution)/shard_map/hand_over/pallas_call | solution.py:450

commit v3 on v2

--- a/solution.py
+++ b/solution.py
@@ -13,10 +13,11 @@
 ORDER = (2, 1, 3, 0)
 NT = (((1,), (1,)), ((), ()))
 STEPS = (
-    "start", "first", "kc_relay", "first_spread", "relay0", "second", "relay-", "kc_last", "relay+", "kc_all",
-    "m0", "relay2", "y0", "m1", "early", "z0", "y1", "m2", "z1", "y2", "last0", "last-", "last+",
-    "m3", "z2", "last2", "y3", "late", "token_grad", "weight_grad",
+    "start", "first", "kc_relay", "know0", "first_spread", "relay0", "know1", "second", "relay-", "kc_last", "kc_all",
+    "m0", "relay+", "know2", "y0", "m1", "relay2", "early", "z0", "y1", "m2", "z1", "y2", "last0", "last-", "last+",
+    "m3", "last2", "z2", "late", "token_grad", "weight_grad",
 )
+NEAR = [(2, 2), (2, 1), (2, 3), (1, 2), (3, 2), (1, 1), (1, 3), (3, 1), (3, 3), (2, 0), (0, 2), (0, 1), (0, 3), (1, 0), (3, 0)]
 P1M, P1P, P1A, P1B = 0, 1, 2, 3
 US = (0, -1, 1, 2)
 ROWS, START, CUT = (144, 112), (0, 144), (80, 48)
@@ -29,8 +30,8 @@
 def kernel(
     tokens, gain_in, codes, scales_in, cotangent,
     key_out, tgrad_out, wgrad_out,
-    gain, scales, tok, kc, cod, wf, w, t, kcs, sg, tg, keyb, pf, pb, yr, sf, sb, zr, rb, zh,
-    load_sem, tok_s, tok_r, kc_s, kcx_r, kcd_r, ag_s, ag_r, dd_s, dd_r, rs_s, y_r, z1_r, z2_r, out_sem,
+    gain, scales, mr, tok, kc, cod, wf, w, t, kcs, sg, tg, keyb, pf, pb, yr, sf, sb, zr, rb, zh,
+    load_sem, tok_s, tok_r, kc_s, kcx_r, kcd_r, ag_s, ag_r, dd_s, dd_r, rs_s, y_r, z1_r, z2_r, know, out_sem,
 ):
     node, local = lax.axis_index("node"), lax.axis_index("local")
     x, zhi, c = node // 8, (node // 2) % 4, node % 2
@@ -60,7 +61,6 @@
     greet += [at(dy=e) for e in (1, 2, 3)]
     greet += [at(dz=1), at(dz=-1)]
     greet += [dev(x, y, zhi * 4 + (zlo + e) % 4, c) for e in (1, 2, 3)]
-    greet += [at(dz=4), at(dz=-4)]
     for who in greet:
         pl.semaphore_signal(barrier, inc=1, device_id=who, device_id_type=MESH)
 
@@ -221,6 +221,15 @@
                     pf[o:o + 16, :] = piece_
                     pb[j * 256 + o:j * 256 + o + 16, :] = piece_.astype(BF16)
         sf[j * 64:(j + 1) * 64, :] = pf[pl.ds(pl.multiple_of(y * 64, 64), 64), :]
+        if j == 3:
+            for dy, dz in NEAR:
+                y_, zl = (y + dy) % 4, (zlo + dz) % 4
+                remote(
+                    pb.at[pl.ds(pl.multiple_of(j * 256 + y_ * 64 + zl * 16, 16), 16)],
+                    mr.at[pl.ds((dy * 4 + dz - 1) * 16, 16)],
+                    rs_s, y_r.at[j], dev(x, y_, zhi * 4 + zl, c),
+                )
+            return
         for e in (2, 1, 3):
             y_ = (y + e) % 4
             remote(
@@ -251,6 +260,13 @@
             s = s + zr[j * 48 + e * 16:j * 48 + (e + 1) * 16, :].astype(F32)
         return s
 
+    def near_sum():
+        drain(mr, y_r.at[3])
+        s = sf[pl.ds(pl.multiple_of(3 * 64 + zlo * 16, 16), 16), :]
+        for e in range(15):
+            s = s + mr[e * 16:(e + 1) * 16, :].astype(F32)
+        return s
+
     def z_far(j):
         s = z_sum(j)
         if j == 1:
@@ -276,6 +292,16 @@
             hand(part, 0, 0)
         kc_hand(0)
         ld_gain.wait()
+        tell(0)
+
+    def tell(level):
+        for step in (1, -1):
+            pl.semaphore_signal(know.at[level], inc=1, device_id=at(dz=step), device_id_type=MESH)
+
+    def heard(level):
+        pl.semaphore_wait(know.at[level], 2)
+        if level < 2:
+            tell(level + 1)
 
     def kc_relay():
         drain(kc_of(-1), kcx_r.at[0])
@@ -341,7 +367,7 @@
         tg_copy.start()
 
     def weight_grad():
-        s = z_sum(3)
+        s = near_sum()
         for j in (1, 2):
             drain(zh.at[pl.ds(j * 16, 16)], z2_r.at[j])
             s = s + zh[j * 16:(j + 1) * 16, :].astype(F32)
@@ -365,7 +391,7 @@
         "relay+": lambda: on_parts(relay, 1), "relay2": lambda: on_parts(relay, 2),
         "last0": lambda: on_parts(last, 0), "last-": lambda: on_parts(last, -1),
         "last+": lambda: on_parts(last, 1), "last2": lambda: on_parts(last, 2),
-        "early": early_shards, "late": late_shards, "token_grad": token_grad, "weight_grad": weight_grad,
+        "know0": lambda: heard(0), "know1": lambda: heard(1), "know2": lambda: heard(2), "early": early_shards, "late": late_shards, "token_grad": token_grad, "weight_grad": weight_grad,
     }
     for j in range(4):
         steps[f"m{j}"] = lambda j=j: chunk_matmul(j)
@@ -416,6 +442,7 @@
         scratch_shapes=[
             pltpu.VMEM((1, D), F32),
             pltpu.VMEM((1, 128), F32),
+            pltpu.VMEM((240, KV), BF16),
             pltpu.VMEM((TOK, D), BF16),
             pltpu.VMEM((TOK, KV), BF16),
             pltpu.VMEM((64, 2048), BF16),
@@ -440,6 +467,7 @@
             dma, dma((40,)),
             dma, dma((2,)),
             dma, dma((4,)), dma((4,)), dma((3,)),
+            pltpu.SemaphoreType.REGULAR((3,)),
             dma((2,)),
         ],
         compiler_params=pltpu.CompilerParams(

time: 62.8 us -> 59.6 us (0.949)
  Pallas kernels: 62 us -> 58.3 us
    pallas_call x1, Pallas kernels: 59.5 us -> 55.7 us  [body(): pl.pallas_call(kernel, out_shape=outs, in_specs=[hbm] * 5, out_specs=(hbm...]
where the time goes in v3:
time: 59.6 us; the launch traced here: 58.9 us
  Pallas kernels  58.3 us (98%)
  between operations  0.64 us (1%)
    pallas_call x1, Pallas kernels, body(): pl.pallas_call(kernel, out_shape=outs, in_specs=[hbm] * 5, out_specs=(hbm...  55.7 us
    pallas_call x1, Pallas kernels, body(): pl.pallas_call(hand_over, out_shape=outs, in_specs=[hbm] * 3, out_specs=(...  2.55 us

profile of v3, /device:TPU:1, one launch (start us, length us, event | category | flops | bytes accessed | tf_op | source)
XLA Modules:
  0.0 58.9 jit_solution(715696115437703353)
XLA Ops:
  0.6 55.7 %key_projection.1 = (bf16[128,512]{1,0:T(8,128)(2,1)}, bf16[128,8192]{1,0:T(8,128)(2,1)}, f32[4,2048]{1,0:T(4,128)}) custom-call(bf16[128,8192]{1,0:T(8,128)(2,1)} %tokens.1, f32[1,8192]{1,0:T(1,128)} %bitcast.2, bf16[128,2048]{1,0:T(8,128)(2,1)} %codes.1, f32[1,128]{1,0:T(1,128)} %bitcast.3, bf16[128,512]{1,0:T(8,128)(2,1)} %cotangent.1), custom_call_target="tpu_custom_call" | custom-call | tf_op jit(solution)/shard_map/key_projection/pallas_call | solution.py:437
  56.3 2.6 %hand_over.1 = (bf16[128,512]{1,0:T(8,128)(2,1)}, bf16[128,8192]{1,0:T(8,128)(2,1)}, f32[4,2048]{1,0:T(4,128)}) custom-call(bf16[128,512]{1,0:T(8,128)(2,1)} %get-tuple-element.6.keys, bf16[128,8192]{1,0:T(8,128)(2,1)} %get-tuple-element.7.tgrad, f32[4,2048]{1,0:T(4,128)} %get-tuple-element.8.wgrad), custom_call_target="tpu_custom_call" | custom-call | tf_op jit(solution)/shard_map/hand_over/pallas_call | solution.py:478

commit v4 on v2

--- a/solution.py
+++ b/solution.py
@@ -13,13 +13,13 @@
 ORDER = (2, 1, 3, 0)
 NT = (((1,), (1,)), ((), ()))
 STEPS = (
-    "start", "first", "kc_relay", "first_spread", "relay0", "second", "relay-", "kc_last", "relay+", "kc_all",
-    "m0", "relay2", "y0", "m1", "early", "z0", "y1", "m2", "z1", "y2", "last0", "last-", "last+",
-    "m3", "z2", "last2", "y3", "late", "token_grad", "weight_grad",
+    "start", "first", "kc_relay", "know0", "first_spread", "relay0", "know1", "second", "relay-", "kc_last", "kc_all",
+    "m0", "relay+", "know2", "y0", "m1", "relay2", "early", "z0", "y1", "m2", "z1", "y2",
+    "m3", "last0", "last-", "last+", "z2", "y3", "last2", "late1", "late2", "late3", "token_grad", "weight_grad",
 )
 P1M, P1P, P1A, P1B = 0, 1, 2, 3
 US = (0, -1, 1, 2)
-ROWS, START, CUT = (144, 112), (0, 144), (80, 48)
+ROWS, START, CUT = (160, 96), (0, 160), (80, 48)
 
 
 def p2(u, kind):
@@ -30,7 +30,7 @@
     tokens, gain_in, codes, scales_in, cotangent,
     key_out, tgrad_out, wgrad_out,
     gain, scales, tok, kc, cod, wf, w, t, kcs, sg, tg, keyb, pf, pb, yr, sf, sb, zr, rb, zh,
-    load_sem, tok_s, tok_r, kc_s, kcx_r, kcd_r, ag_s, ag_r, dd_s, dd_r, rs_s, y_r, z1_r, z2_r, out_sem,
+    load_sem, tok_s, tok_r, kc_s, kcx_r, kcd_r, ag_s, ag_r, dd_s, dd_r, rs_s, y_r, z1_r, z2_r, know, out_sem,
 ):
     node, local = lax.axis_index("node"), lax.axis_index("local")
     x, zhi, c = node // 8, (node // 2) % 4, node % 2
@@ -60,7 +60,6 @@
     greet += [at(dy=e) for e in (1, 2, 3)]
     greet += [at(dz=1), at(dz=-1)]
     greet += [dev(x, y, zhi * 4 + (zlo + e) % 4, c) for e in (1, 2, 3)]
-    greet += [at(dz=4), at(dz=-4)]
     for who in greet:
         pl.semaphore_signal(barrier, inc=1, device_id=who, device_id_type=MESH)
 
@@ -125,8 +124,8 @@
     def hand(part, du, dv):
         dy, dz = uv(part, du, dv)
         ref = piece(dy, dz, part)
-        late = dy == 2 or dz == 2
-        remote(ref, ref, dd_s, dd_r.at[1 if late else 0], partner)
+        group = 0 if 2 not in (dy, dz) else 1 if 0 in (dy, dz) else 3 if dy == dz else 2
+        remote(ref, ref, dd_s, dd_r.at[group], partner)
 
     def spread(part, du):
         ag_send(part, du, 0, 1, 1, p2(du, 0))
@@ -276,6 +275,16 @@
             hand(part, 0, 0)
         kc_hand(0)
         ld_gain.wait()
+        tell(0)
+
+    def tell(level):
+        for step in (1, -1):
+            pl.semaphore_signal(know.at[level], inc=1, device_id=at(dz=step), device_id_type=MESH)
+
+    def heard(level):
+        pl.semaphore_wait(know.at[level], 2)
+        if level < 2:
+            tell(level + 1)
 
     def kc_relay():
         drain(kc_of(-1), kcx_r.at[0])
@@ -318,13 +327,21 @@
         drain(w.at[pl.ds(0, 9 * 256)], dd_r.at[0])
         shards(9, lambda i: (i % 3 - 1, i // 3 - 1))
 
-    def late_shards():
-        drain(w.at[pl.ds(0, 7 * 256)], dd_r.at[1])
-        shards(4, lambda i: (2, i - 1))
-        shards(3, lambda i: (i - 1, 2))
+    def late_shards(group):
+        drain(w.at[pl.ds(0, (2, 4, 1)[group - 1] * 256)], dd_r.at[group])
+        if group == 1:
+            shards(2, lambda i: (2 * i, 2 - 2 * i))
+        elif group == 2:
+            shards(2, lambda i: (2 * i - 1, 2))
+            shards(2, lambda i: (2, 2 * i - 1))
+        else:
+            shards(1, lambda i: (2, 2))
 
     key_copy = pltpu.make_async_copy(keyb, key_out, out_sem.at[0])
-    tg_copy = pltpu.make_async_copy(tg, tgrad_out, out_sem.at[1])
+    tg_copies = []
+    for q in range(4):
+        quarter = pl.ds(q * 2048, 2048)
+        tg_copies.append(pltpu.make_async_copy(tg.at[:, quarter], tgrad_out.at[:, quarter], out_sem.at[1 + q]))
 
     def token_grad():
         keyb[...] = state["keys"].astype(BF16)
@@ -337,8 +354,9 @@
             tg[:, cs] = (inv * (sg[:, cs] - tok[:, cs].astype(F32) * coef)).astype(BF16)
             return 0
 
-        lax.fori_loop(0, 16, final, 0)
-        tg_copy.start()
+        for q in range(4):
+            lax.fori_loop(4 * q, 4 * q + 4, final, 0)
+            tg_copies[q].start()
 
     def weight_grad():
         s = z_sum(3)
@@ -365,7 +383,7 @@
         "relay+": lambda: on_parts(relay, 1), "relay2": lambda: on_parts(relay, 2),
         "last0": lambda: on_parts(last, 0), "last-": lambda: on_parts(last, -1),
         "last+": lambda: on_parts(last, 1), "last2": lambda: on_parts(last, 2),
-        "early": early_shards, "late": late_shards, "token_grad": token_grad, "weight_grad": weight_grad,
+        "know0": lambda: heard(0), "know1": lambda: heard(1), "know2": lambda: heard(2), "early": early_shards, "late1": lambda: late_shards(1), "late2": lambda: late_shards(2), "late3": lambda: late_shards(3), "token_grad": token_grad, "weight_grad": weight_grad,
     }
     for j in range(4):
         steps[f"m{j}"] = lambda j=j: chunk_matmul(j)
@@ -375,7 +393,8 @@
         steps[step]()
 
     key_copy.wait()
-    tg_copy.wait()
+    for tg_copy in tg_copies:
+        tg_copy.wait()
     drain(t.at[pl.ds(0, 3584)], tok_s)
     drain(kcs.at[pl.ds(0, 896)], kc_s)
     drain(w.at[pl.ds(0, 3840)], ag_s)
@@ -438,9 +457,10 @@
             dma, dma((4,)),
             dma, dma((4,)), dma,
             dma, dma((40,)),
-            dma, dma((2,)),
+            dma, dma((4,)),
             dma, dma((4,)), dma((4,)), dma((3,)),
-            dma((2,)),
+            pltpu.SemaphoreType.REGULAR((3,)),
+            dma((5,)),
         ],
         compiler_params=pltpu.CompilerParams(
             collective_id=0, has_side_effects=True, vmem_limit_bytes=62 * 1024 * 1024

time: 62.8 us -> 59.3 us (0.944)
  Pallas kernels: 62 us -> 58.5 us
    pallas_call x1, Pallas kernels: 59.5 us -> 56 us  [body(): pl.pallas_call(kernel, out_shape=outs, in_specs=[hbm] * 5, out_specs=(hbm...]
where the time goes in v4:
time: 59.3 us; the launch traced here: 59.2 us
  Pallas kernels  58.5 us (99%)
  between operations  0.64 us (1%)
    pallas_call x1, Pallas kernels, body(): pl.pallas_call(kernel, out_shape=outs, in_specs=[hbm] * 5, out_specs=(hbm...  56 us
    pallas_call x1, Pallas kernels, body(): pl.pallas_call(hand_over, out_shape=outs, in_specs=[hbm] * 3, out_specs=(...  2.55 us

profile of v4, /device:TPU:1, one launch (start us, length us, event | category | flops | bytes accessed | tf_op | source)
XLA Modules:
  0.0 59.2 jit_solution(14866443890768382078)
XLA Ops:
  0.6 56.0 %key_projection.1 = (bf16[128,512]{1,0:T(8,128)(2,1)}, bf16[128,8192]{1,0:T(8,128)(2,1)}, f32[4,2048]{1,0:T(4,128)}) custom-call(bf16[128,8192]{1,0:T(8,128)(2,1)} %tokens.1, f32[1,8192]{1,0:T(1,128)} %bitcast.2, bf16[128,2048]{1,0:T(8,128)(2,1)} %codes.1, f32[1,128]{1,0:T(1,128)} %bitcast.3, bf16[128,512]{1,0:T(8,128)(2,1)} %cotangent.1), custom_call_target="tpu_custom_call" | custom-call | tf_op jit(solution)/shard_map/key_projection/pallas_call | solution.py:430
  56.6 2.6 %hand_over.1 = (bf16[128,512]{1,0:T(8,128)(2,1)}, bf16[128,8192]{1,0:T(8,128)(2,1)}, f32[4,2048]{1,0:T(4,128)}) custom-call(bf16[128,512]{1,0:T(8,128)(2,1)} %get-tuple-element.6.keys, bf16[128,8192]{1,0:T(8,128)(2,1)} %get-tuple-element.7.tgrad, f32[4,2048]{1,0:T(4,128)} %get-tuple-element.8.wgrad), custom_call_target="tpu_custom_call" | custom-call | tf_op jit(solution)/shard_map/hand_over/pallas_call | solution.py:470

commit v5 on v4

--- a/solution.py
+++ b/solution.py
@@ -13,7 +13,7 @@
 ORDER = (2, 1, 3, 0)
 NT = (((1,), (1,)), ((), ()))
 STEPS = (
-    "start", "first", "kc_relay", "know0", "first_spread", "relay0", "know1", "second", "relay-", "kc_last", "kc_all",
+    "start", "first", "kc_relay", "know0", "first_spread", "relay0", "tok_rest", "know1", "second", "relay-", "kc_last", "kc_all",
     "m0", "relay+", "know2", "y0", "m1", "relay2", "early", "z0", "y1", "m2", "z1", "y2",
     "m3", "last0", "last-", "last+", "z2", "y3", "last2", "late1", "late2", "late3", "token_grad", "weight_grad",
 )
@@ -264,12 +264,12 @@
 
     def start():
         pl.semaphore_wait(barrier, len(greet))
+        for part in (0, 1):
+            ag_send(part, 0, 0, 0, 1, P1M)
+            ag_send(part, 0, 0, 0, -1, P1P)
         kc_send(0, 1, 0)
         kc_send(0, -1, 1)
         tok_send(0)
-        for part in (0, 1):
-            ag_send(part, 0, 0, 0, 1, P1M)
-            ag_send(part, 0, 0, 0, -1, P1P)
         for part in (0, 1):
             spread(part, 0)
             hand(part, 0, 0)
@@ -291,10 +291,13 @@
         kc_send(-1, 1, 2, 0)
         drain(kc_of(1), kcx_r.at[1])
         kc_send(1, -1, 3, 1)
-        for j in (1, 2, 3):
-            tok_send(j)
+        tok_send(1)
         kc_hand(-1)
         kc_hand(1)
+
+    def tok_rest():
+        tok_send(2)
+        tok_send(3)
 
     def kc_last():
         drain(kc_of(2, 0), kcx_r.at[2])
@@ -375,7 +378,7 @@
             step(part, *args)
 
     steps = {
-        "start": start, "kc_relay": kc_relay, "kc_last": kc_last,
+        "start": start, "tok_rest": tok_rest, "kc_relay": kc_relay, "kc_last": kc_last,
         "kc_all": lambda: drain(kcs.at[pl.ds(0, 512)], kcd_r),
         "first": lambda: on_parts(first), "first_spread": lambda: on_parts(first_spread),
         "second": lambda: on_parts(second),
@@ -404,8 +407,8 @@
 
 def hand_over(keys, tgrad, wgrad, keys_out, tgrad_out, wgrad_out, kv, tv, wv, sem_in, sem_out):
     parts = [(keys, kv, keys_out), (wgrad, wv, wgrad_out)]
-    for i in range(4):
-        rows = pl.ds(i * 32, 32)
+    for i in range(8):
+        rows = pl.ds(i * 16, 16)
         parts.append((tgrad.at[rows], tv.at[rows], tgrad_out.at[rows]))
     loads = [pltpu.make_async_copy(src, mid, sem_in.at[i]) for i, (src, mid, _) in enumerate(parts)]
     stores = [pltpu.make_async_copy(mid, dst, sem_out.at[i]) for i, (_, mid, dst) in enumerate(parts)]
@@ -476,8 +479,8 @@
             pltpu.VMEM((TOK, KV), BF16),
             pltpu.VMEM((TOK, D), BF16),
             pltpu.VMEM((4, 2048), F32),
-            dma((6,)),
-            dma((6,)),
+            dma((10,)),
+            dma((10,)),
         ],
         compiler_params=pltpu.CompilerParams(vmem_limit_bytes=62 * 1024 * 1024),
         name="hand_over",

time: 59.3 us -> 59.3 us (level)
  no operation moved by 1% of the time
where the time goes in v5:
time: 59.3 us; the launch traced here: 59.1 us
  Pallas kernels  58.5 us (99%)
  between operations  0.64 us (1%)
    pallas_call x1, Pallas kernels, body(): pl.pallas_call(kernel, out_shape=outs, in_specs=[hbm] * 5, out_specs=(hbm...  56 us
    pallas_call x1, Pallas kernels, body(): pl.pallas_call(hand_over, out_shape=outs, in_specs=[hbm] * 3, out_specs=(...  2.52 us

profile of v5, /device:TPU:1, one launch (start us, length us, event | category | flops | bytes accessed | tf_op | source)
XLA Modules:
  0.0 59.1 jit_solution(8935180732615544323)
XLA Ops:
  0.6 56.0 %key_projection.1 = (bf16[128,512]{1,0:T(8,128)(2,1)}, bf16[128,8192]{1,0:T(8,128)(2,1)}, f32[4,2048]{1,0:T(4,128)}) custom-call(bf16[128,8192]{1,0:T(8,128)(2,1)} %tokens.1, f32[1,8192]{1,0:T(1,128)} %bitcast.2, bf16[128,2048]{1,0:T(8,128)(2,1)} %codes.1, f32[1,128]{1,0:T(1,128)} %bitcast.3, bf16[128,512]{1,0:T(8,128)(2,1)} %cotangent.1), custom_call_target="tpu_custom_call" | custom-call | tf_op jit(solution)/shard_map/key_projection/pallas_call | solution.py:433
  56.6 2.5 %hand_over.1 = (bf16[128,512]{1,0:T(8,128)(2,1)}, bf16[128,8192]{1,0:T(8,128)(2,1)}, f32[4,2048]{1,0:T(4,128)}) custom-call(bf16[128,512]{1,0:T(8,128)(2,1)} %get-tuple-element.6.keys, bf16[128,8192]{1,0:T(8,128)(2,1)} %get-tuple-element.7.tgrad, f32[4,2048]{1,0:T(4,128)} %get-tuple-element.8.wgrad), custom_call_target="tpu_custom_call" | custom-call | tf_op jit(solution)/shard_map/hand_over/pallas_call | solution.py:473
